TPU v7x, 128 devices: a whole 4x4x4 slice. The times are simulated.
128 devices in a mesh: sample: 4 (over z), cent: 32 (over x, y, core).
Axes of the slice: x: 4, y: 4, z: 4, core: 2. Of those that a mesh axis runs over, the one named last changes fastest.
Arguments:
- embeddings: bfloat16 [2097152, 256], P(('sample', 'cent')), may hold values from -6 to 6
- route: int32 [2097152, 1], P(('sample', 'cent')), may hold values from 0 to 127; in each aligned block of 16384 rows (0 to 16383, 16384 to 32767, ...) at most 256 rows name the same one
- offset: int32 [2097152], P(('sample', 'cent')), may hold values from 0 to 511
- centroids: float32 [65536, 256], P('cent'), may hold values from -6 to 6
Outputs:
- updated: float32 [65536, 256], P('cent')
Inputs may be any that keep to these rules, and one draw needn't show every extreme that they name: Of the 16384 rows of one device (aligned blocks), at most 256 name one route; route r holds centroids r * 512 to (r + 1) * 512 - 1.
All inputs are finite; a program needn't handle non-finite values.
Results may differ from a plain program's by a relative error of at most 0.0003.
Values may be sent and summed in bfloat16 or wider, within the bound.
A program may use at most 128 MiB of HBM per device.

v0:
```python
import jax
import jax.numpy as jnp
from jax import lax
from jax.sharding import PartitionSpec as P

K = 65536


def ranks_within(target, groups):
    marks = (target[:, None] == jnp.arange(groups, dtype=jnp.int32)[None, :]).astype(jnp.int32)
    running = jnp.cumsum(marks, axis=0) - 1
    return jnp.sum(running * marks, axis=1)


def fill_slots(embeddings, offset, slots, total):
    width = embeddings.shape[1]
    buffer = jnp.zeros((total, width), jnp.bfloat16).at[slots].set(embeddings)
    labels = jnp.full((total,), -1, jnp.int32).at[slots].set(offset)
    return (buffer, labels)


def local(embeddings, route, offset, centroids):
    n_sample = lax.axis_size("sample")
    n_cent = lax.axis_size("cent")
    devices = n_sample * n_cent
    rows = embeddings.shape[0]
    width = embeddings.shape[1]
    sub = K // devices
    cap = 2 * rows // devices
    target = route[:, 0]
    rank = ranks_within(target, devices)
    quarter = lax.axis_index("sample")
    slots = target // n_sample * (n_sample * cap) + target % n_sample * cap + rank
    buffer, labels = fill_slots(embeddings, offset, slots, devices * cap)
    buffer = buffer.reshape(n_cent, n_sample * cap, width)
    labels = labels.reshape(n_cent, n_sample * cap)
    got_rows, got_labels = (
        lax.all_to_all(buffer, "cent", split_axis=0, concat_axis=0, tiled=True),
        lax.all_to_all(labels, "cent", split_axis=0, concat_axis=0, tiled=True),
    )
    got_rows = got_rows.reshape(n_cent, n_sample, cap, width)
    got_labels = got_labels.reshape(n_cent, n_sample, cap)
    onehot = (got_labels[..., None] == jnp.arange(sub, dtype=jnp.int32)).astype(jnp.bfloat16)
    partial_value = jnp.einsum(
        "ansk,ansd->nkd", onehot, got_rows, preferred_element_type=jnp.float32
    )
    tallies = jnp.sum(onehot, axis=(0, 2), dtype=jnp.float32)
    sums, counts = (
        lax.psum_scatter(
            partial_value.reshape(n_sample * sub, width), "sample", scatter_dimension=0, tiled=True
        ),
        lax.psum_scatter(
            tallies.reshape(n_sample * sub), "sample", scatter_dimension=0, tiled=True
        ),
    )
    previous = lax.dynamic_slice_in_dim(centroids, quarter * sub, sub, 0)
    safe = jnp.maximum(counts, 1.0)
    fresh = jnp.where(counts[:, None] > 0.0, sums / safe[:, None], previous)
    return lax.all_gather(fresh, "sample", axis=0, tiled=True)


def solution(mesh):
    in_specs = (
        P(("sample", "cent"), None),
        P(("sample", "cent"), None),
        P(("sample", "cent")),
        P("cent", None),
    )
    out_specs = P("cent", None)
    return jax.shard_map(local, mesh=mesh, in_specs=in_specs, out_specs=out_specs, check_vma=False)
```

profile of v0, /device:TPU:0, one launch (start us, length us, event | category | flops | bytes accessed | tf_op | source)
XLA Modules:
  0.0 550.1 jit_solution(17569698555184508757)
XLA Ops:
  6.5 0.9 copy.14
  7.5 1.0 fusion.7
  8.5 0.0 copy-start
  8.5 3.2 copy-done
  11.7 0.1 copy.15
  11.8 0.2 reduce-window.9
  12.0 0.1 copy.16
  12.1 8.4 %add_add_fusion = s32[128,128,128]{1,0,2:T(8,128)} fusion(s32[128,128,128]{1,0,2:T(8,128)} %copy-done, s32[128,128]{1,0:T(8,128)S(1)} %copy.16), kind=kLoop, calls=%fused_computation.12 | loop fusion | flops 4194304 | bytes 16842752 | tf_op jit(solution)/shard_map/sub | solution.py:11
  20.5 0.0 copy-start.1
  20.5 9.3 %copy.17 = s32[128,128,128]{0,2,1:T(8,128)} copy(s32[128,128,128]{1,0,2:T(8,128)} %add_add_fusion) | data formatting | bytes 16777216 | tf_op jit(solution)/shard_map/sub | solution.py:11
  29.8 0.0 copy-done.1
  29.8 8.3 %fusion.4 = s32[16384]{0:T(1024)S(1)} fusion(s32[128,128,128]{0,2,1:T(8,128)} %copy.17, s32[16384]{0:T(1024)S(1)} %bitcast.29), kind=kLoop, calls=%fused_computation.9 | loop fusion | flops 6275072 | bytes 8519680 | tf_op jit(solution)/shard_map/reduce_sum | solution.py:12
  38.1 0.6 compare_select_fusion
  38.7 61.2 %scatter_custom_fusion = s32[32768]{0:T(1024)} fusion(s32[16384]{0:T(1024)S(1)} %bitcast.34, s32[16384]{0:T(1024)} %param.6, s32[]{:T(128)} %constant.44.clone.1), kind=kCustom, calls=%fused_computation.30 | custom fusion | bytes 131584 | tf_op jit(solution)/shard_map/scatter | solution.py:18
  99.8 7.4 %all-to-all-start = ((s32[32,1,1024]{2,1,0:T(1,128)}), s32[32,1,1024]{2,1,0:T(1,128)S(1)}, u32[]{:S(2)}, u32[]{:S(2)}) async-start(s32[32,1,1024]{2,1,0:T(1,128)} %bitcast.7), calls=%async_computation | async-start | bytes 262144 | tf_op jit(solution)/shard_map/all_to_all | solution.py:39
  107.2 78.5 %scatter_custom_fusion.1 = bf16[32768,256]{1,0:T(8,128)(2,1)} fusion(s32[16384]{0:T(1024)S(1)} %bitcast.35, bf16[16384,256]{1,0:T(8,128)(2,1)} %param.4, bf16[]{:T(256)} %constant.54.clone.1), kind=kCustom, calls=%fused_computation.10 | custom fusion | bytes 16777728 | tf_op jit(solution)/shard_map/scatter | solution.py:17
  185.8 0.0 all-to-all-done
  185.8 7.5 %all-to-all-start.1 = ((bf16[32,1024,256]{2,1,0:T(8,128)(2,1)}), bf16[32,1024,256]{2,1,0:T(8,128)(2,1)}, u32[]{:S(2)}, u32[]{:S(2)}) async-start(bf16[32,1024,256]{2,1,0:T(8,128)(2,1)} %bitcast.26), calls=%async_computation.1 | async-start | bytes 33554432 | tf_op jit(solution)/shard_map/all_to_all | solution.py:38
  193.3 0.0 reduce-scatter.2.cloned.1.call-start
  193.4 0.3 reduce
  193.7 240.5 %all-to-all-done.1 = bf16[32,1024,256]{2,1,0:T(8,128)(2,1)} async-done(((bf16[32,1024,256]{2,1,0:T(8,128)(2,1)}), bf16[32,1024,256]{2,1,0:T(8,128)(2,1)}, u32[]{:S(2)}, u32[]{:S(2)}) %all-to-all-start.1) | async-done | bytes 16777248 | tf_op jit(solution)/shard_map/all_to_all | solution.py:38
  434.2 0.0 copy-start.2
  434.2 13.3 %fusion = f32[4,512,256,1]{2,1,3,0:T(8,128)} fusion(s32[32,4,256]{2,0,1:T(8,128)S(1)} %bitcast.32, bf16[32,4,256,256]{3,2,1,0:T(8,128)(2,1)} %bitcast.9), kind=kOutput, calls=%fused_computation.4 | convolution fusion | flops 8606711808 | bytes 19005440 | tf_op jit(solution)/shard_map/ansk,ansd->nkd/dot_general | solution.py:44
  447.5 0.0 reduce-scatter.2.cloned.1.call-update
  447.5 0.0 all-gather.2.cloned.1.call-start
  447.6 0.0 copy-done.2
  447.6 0.7 dynamic-slice
  449.0 8.0 %convert_reduce_fusion = f32[4,512]{1,0:T(4,128)S(1)} fusion(s32[32,4,256]{2,0,1:T(8,128)S(1)} %bitcast.33), kind=kLoop, calls=%fused_computation.2 | loop fusion | flops 67106816 | bytes 139264 | tf_op jit(solution)/shard_map/reduce_sum | solution.py:47
  457.0 11.9 %all-reduce = f32[2048]{0:T(1024)S(1)} all-reduce(f32[2048]{0:T(1024)S(1)} %bitcast.36), channel_id=2, replica_groups=mesh['sample'=4,'cent'=32] {'sample'}, use_global_device_ids=true, to_apply=%region_5.6.clone | all-reduce | flops 2048 | bytes 16384
  468.9 0.1 dynamic-slice_compare_fusion
  469.0 0.1 dynamic-slice_maximum_fusion
  469.0 38.2 %reduce-scatter.2.cloned.1.call-done = f32[512,256]{1,0:T(8,128)} async-done(((f32[2048,256]{1,0:T(8,128)}), f32[512,256]{1,0:T(8,128)}) %reduce-scatter.2.cloned.1.call-update) | async-done | bytes 524304 | tf_op jit(solution)/shard_map/reduce_scatter | solution.py:49
  507.2 2.2 dynamic-slice_select_fusion
  509.4 0.0 all-gather.2.cloned.1.call-update
  509.5 30.8 %all-gather.2.cloned.1.call-done = f32[2048,256]{1,0:T(8,128)} async-done(((f32[512,256]{1,0:T(8,128)}), f32[2048,256]{1,0:T(8,128)}) %all-gather.2.cloned.1.call-update) | async-done | bytes 2097168 | tf_op jit(solution)/shard_map/all_gather | solution.py:59
  540.3 3.0 copy.28
  (4 shorter events, 0.0 us)
Async XLA Ops:
  8.5 3.2 copy-start
  20.5 9.3 %copy-start.1 = (s32[16384,1]{0,1:T(1,128)S(1)}, s32[16384,1]{0,1:T(1,128)}, u32[]{:S(2)}) copy-start(s32[16384,1]{0,1:T(1,128)} %param.5) | copy-start | bytes 196612
  99.8 86.0 %all-to-all-start = ((s32[32,1,1024]{2,1,0:T(1,128)}), s32[32,1,1024]{2,1,0:T(1,128)S(1)}, u32[]{:S(2)}, u32[]{:S(2)}) async-start(s32[32,1,1024]{2,1,0:T(1,128)} %bitcast.7), calls=%async_computation | async-start | bytes 262144 | tf_op jit(solution)/shard_map/all_to_all | solution.py:39
  185.8 248.4 %all-to-all-start.1 = ((bf16[32,1024,256]{2,1,0:T(8,128)(2,1)}), bf16[32,1024,256]{2,1,0:T(8,128)(2,1)}, u32[]{:S(2)}, u32[]{:S(2)}) async-start(bf16[32,1024,256]{2,1,0:T(8,128)(2,1)} %bitcast.26), calls=%async_computation.1 | async-start | bytes 33554432 | tf_op jit(solution)/shard_map/all_to_all | solution.py:38
  193.3 313.9 %reduce-scatter.2.cloned.1.call-start = ((), (), s32[]{:S(2)}) async-start(), calls=%async_computation.3 | async-start | bytes 2621440 | tf_op jit(solution)/shard_map/reduce_scatter | solution.py:49
  434.2 13.4 %copy-start.2 = (u32[128]{0:T(128)S(1)}, u32[128]{0:T(128)}, u32[]{:S(2)}) copy-start(u32[128]{0:T(128)} %constant.62) | copy-start | bytes 1540
  447.5 92.7 %all-gather.2.cloned.1.call-start = ((), (), s32[]{:S(2)}) async-start(), calls=%async_computation.4 | async-start | bytes 2621440 | tf_op jit(solution)/shard_map/all_gather | solution.py:59
Sparse Core Ops, SparseCore 0:
  447.7 59.5 reduce-scatter.1
  509.6 30.6 all-gather.1
where the time goes:
time: 552 us; the launch traced here: 550 us
  waiting for transfers between devices  310 us (56%)
  local copies, waits for them, and re-layouts  157 us (28%)
  other arithmetic  29.1 us (5%)
  starting transfers between devices  15 us (3%)
  between operations  14.2 us (3%)
  matrix products  13.3 us (2%)
  blocking collectives  11.9 us (2%)
    all_to_all x1, waiting for transfers between devices, local(): lax.all_to_all(buffer, 'cent', split_axis=0, concat_axis=0, tiled=True)  241 us
    scatter x1, local copies, waits for them, and re-layouts, fill_slots(): buffer = jnp.zeros((total, width), jnp.bfloat16).at[slots].set(embeddings)  78.5 us
    scatter x1, local copies, waits for them, and re-layouts, fill_slots(): labels = jnp.full((total,), -1, jnp.int32).at[slots].set(offset)  61.2 us
    reduce_scatter x1, waiting for transfers between devices, local(): lax.psum_scatter(partial_value.reshape(n_sample * sub, width), 'sample',...  38.2 us
    all_gather x1, waiting for transfers between devices, local(): return lax.all_gather(fresh, 'sample', axis=0, tiled=True)  30.8 us
    dot_general x1, matrix products, local(): jnp.einsum('ansk,ansd->nkd', onehot, got_rows, preferred_element_type=jnp...  13.3 us
    unnamed x1, blocking collectives  11.9 us
  transfers between devices with their start and end apart: 4, of which 3 were waited for; matrix products, arithmetic and copies ran while one was open for 16% of the time, Pallas kernels for 0%

commit v1 on v0

v1 whole, which is shorter than its diff:
```python
import functools

import jax
import jax.numpy as jnp
from jax import lax
from jax.experimental import pallas as pl
from jax.experimental.pallas import tpu as pltpu
from jax.sharding import PartitionSpec as P

MESH = pl.DeviceIdType.MESH
K = 65536
WIDTH = 256
ROUTES = 128
SUB = 512
CAP = 256
ROWS = 16384
CHUNK = 512
CHUNKS = ROWS // CHUNK
SLOTS = ROUTES * CAP
PART = 1024
F32, BF16, I32 = jnp.float32, jnp.bfloat16, jnp.int32


def place_of(route):
    quarter = route & 3
    core = (route >> 2) & 1
    y = (route >> 3) & 3
    x = route >> 5
    by_y = (quarter == 1) | ((quarter == 3) & (core == 1))
    ring = jnp.where(by_y, y, x)
    other = jnp.where(by_y, x, y)
    return quarter * 32 + ring * 8 + core * 4 + other


def index_kernel(route, offset, x, slots, labels, counts, pairs, upper, weave, base, found):
    step = pl.program_id(0)

    @pl.when(step == 0)
    def _():
        row = lax.broadcasted_iota(I32, (CHUNK, CHUNK), 0)
        col = lax.broadcasted_iota(I32, (CHUNK, CHUNK), 1)
        upper[...] = (row < col).astype(F32).astype(BF16)
        row = lax.broadcasted_iota(I32, (256, 256), 0)
        col = lax.broadcasted_iota(I32, (256, 256), 1)
        weave[...] = (col == (row >> 1) + (row & 1) * 128).astype(F32).astype(BF16)
        base[...] = jnp.zeros_like(base)
        found[...] = jnp.zeros_like(found)
        counts[...] = jnp.zeros_like(counts)

    named = route[pl.ds(step, 1), :]
    within = offset[pl.ds(step, 1), :]
    place = place_of(named)
    lane_dot = (((1,), (1,)), ((), ()))

    routes = lax.broadcasted_iota(I32, (ROUTES, CHUNK), 0)
    mark = routes == place
    mark_f = mark.astype(F32)
    mark_b = mark_f.astype(BF16)
    before = jnp.dot(mark_b, upper[...], preferred_element_type=F32) + base[:, :1]
    rank = jnp.sum(jnp.where(mark, before, 0.0), axis=0, keepdims=True).astype(I32)
    slots[pl.ds(step, 1), :] = place * CAP + rank
    base[...] = base[...] + jnp.sum(mark_f, axis=1, keepdims=True)

    ranks = lax.broadcasted_iota(I32, (CAP, CHUNK), 0)
    value = jnp.where(ranks == rank, (within - 256).astype(F32), 0.0).astype(BF16)
    found[...] += lax.dot_general(mark_b, value, lane_dot, preferred_element_type=F32)

    natural = (routes == named).astype(F32).astype(BF16)
    offsets = lax.broadcasted_iota(I32, (SUB, CHUNK), 0)
    hit = (offsets == within).astype(F32).astype(BF16)
    counts[...] += lax.dot_general(natural, hit, lane_dot, preferred_element_type=F32)

    for part in range(CHUNK // 128):
        block = x[part * 128:(part + 1) * 128, :]
        stacked = jnp.concatenate([block[:, :128], block[:, 128:]], axis=0)
        woven = jnp.dot(weave[...], stacked, preferred_element_type=F32)
        pairs[part * 256:(part + 1) * 256, :] = woven.astype(BF16)

    @pl.when(step == CHUNKS - 1)
    def _():
        lanes = lax.broadcasted_iota(I32, (ROUTES, CAP), 1)
        labels[...] = jnp.where(lanes < base[:, :1].astype(I32), found[...].astype(I32) + 256, -1)


def index_call(route, offset, x):
    whole = lambda shape: pl.BlockSpec(shape, lambda i: (0,) * len(shape))
    return pl.pallas_call(
        index_kernel,
        grid=(CHUNKS,),
        out_shape=[
            jax.ShapeDtypeStruct((CHUNKS, CHUNK), I32),
            jax.ShapeDtypeStruct((ROUTES, CAP), I32),
            jax.ShapeDtypeStruct((ROUTES, SUB), F32),
            jax.ShapeDtypeStruct((2 * ROWS, 128), BF16),
        ],
        in_specs=[
            whole((CHUNKS, CHUNK)),
            whole((CHUNKS, CHUNK)),
            pl.BlockSpec((CHUNK, WIDTH), lambda i: (i, 0)),
        ],
        out_specs=[
            whole((CHUNKS, CHUNK)),
            whole((ROUTES, CAP)),
            whole((ROUTES, SUB)),
            pl.BlockSpec((2 * CHUNK, 128), lambda i: (i, 0)),
        ],
        scratch_shapes=[
            pltpu.VMEM((CHUNK, CHUNK), BF16),
            pltpu.VMEM((256, 256), BF16),
            pltpu.VMEM((ROUTES, 128), F32),
            pltpu.VMEM((ROUTES, CAP), F32),
        ],
        compiler_params=pltpu.CompilerParams(vmem_limit_bytes=32 << 20),
    )(route, offset, x)


def place_kernel(slots, x, out, rows, packed, blank, in_sem, zero_sem, out_sem):
    loads = []
    for part in range(ROWS // PART):
        span = pl.ds(part * PART, PART)
        loads.append(pltpu.make_async_copy(x.at[span], rows.at[span], in_sem.at[part]))
        loads[-1].start()
    blank[...] = jnp.zeros_like(blank)
    clears = []
    for part in range(SLOTS // PART):
        clears.append(pltpu.make_async_copy(blank, packed.at[pl.ds(part * PART, PART)], zero_sem.at[part]))
        clears[-1].start()
    for clear in clears:
        clear.wait()
    for part, load in enumerate(loads):
        load.wait()

        def sixteen(i, _):
            for u in range(16):
                j = part * PART + i * 16 + u
                packed[slots[j]] = rows[j]
            return 0

        lax.fori_loop(0, PART // 16, sixteen, 0)
    stores = []
    for part in range(SLOTS // PART):
        span = pl.ds(part * PART, PART)
        stores.append(pltpu.make_async_copy(packed.at[span], out.at[span], out_sem.at[part]))
        stores[-1].start()
    for store in stores:
        store.wait()


def place_call(slots, x):
    return pl.pallas_call(
        place_kernel,
        out_shape=jax.ShapeDtypeStruct((SLOTS, 2, 128), BF16),
        in_specs=[pl.BlockSpec(memory_space=pltpu.SMEM), pl.BlockSpec(memory_space=pl.ANY)],
        out_specs=pl.BlockSpec(memory_space=pl.ANY),
        scratch_shapes=[
            pltpu.VMEM((ROWS, 2, 128), BF16),
            pltpu.VMEM((SLOTS, 2, 128), BF16),
            pltpu.VMEM((PART, 2, 128), BF16),
            pltpu.SemaphoreType.DMA((ROWS // PART,)),
            pltpu.SemaphoreType.DMA((SLOTS // PART,)),
            pltpu.SemaphoreType.DMA((SLOTS // PART,)),
        ],
        compiler_params=pltpu.CompilerParams(vmem_limit_bytes=56 << 20),
    )(slots, x)


def device_at(x, y, z, core):
    return {"sample": z, "cent": (x * 4 + y) * 2 + core}


def reduce_kernel(rows, labels, out, got, got_labels, partial, got2, second, got3, third, crossed,
                  s1, r1, sl, rl, s2, r2, s3, r3, s4, r4, s5, r5, own):
    z = lax.axis_index("sample")
    cent = lax.axis_index("cent")
    x, y, core = cent // 8, (cent // 2) % 4, cent % 2
    at = {"x": x, "y": y, "z": z}

    def along(axis, distance, core_to=None):
        to = dict(at)
        to[axis] = (to[axis] + distance) % 4
        return device_at(to["x"], to["y"], to["z"], core if core_to is None else core_to)

    def by_core(distance):
        return device_at((x + distance * core) % 4, (y + distance * (1 - core)) % 4, z, core)

    barrier = pltpu.get_barrier_semaphore()
    other = (core + 1) % 2
    pl.semaphore_signal(barrier, inc=1, device_id=device_at(x, y, z, other), device_id_type=MESH)
    for axis in "xyz":
        for distance in (1, 2, 3):
            for core_to in (core, other):
                pl.semaphore_signal(barrier, inc=1, device_id=along(axis, distance, core_to), device_id_type=MESH)
    pl.semaphore_wait(barrier, 19)

    hops = [(2, 0), (2, 1), (1, 0), (3, 0), (1, 1), (3, 1), (0, 1)]
    first = {}
    for j, (distance, flip) in enumerate(hops):
        for q in (2, 0, 1, 3):
            core_to = (core + flip) % 2
            if q == 3:
                ring = x * (1 - core_to) + y * core_to
                device = device_at((x + distance * (1 - core_to)) % 4, (y + distance * core_to) % 4, z, core_to)
            else:
                axis = "xyz"[q]
                ring = at[axis]
                device = along(axis, distance, core_to)
            to = ((ring + distance) % 4) * 2 + core_to
            mine = ring * 2 + core
            pair = []
            for src, dst, ss, rs in ((rows, got, s1, r1), (labels, got_labels, sl, rl)):
                pair.append(pltpu.make_async_remote_copy(
                    src_ref=src.at[q, to], dst_ref=dst.at[q, mine], send_sem=ss.at[q, j], recv_sem=rs.at[q, j],
                    device_id=device, device_id_type=MESH))
                pair[-1].start()
            first[q, j] = pair
    local = {}
    for q in range(4):
        ring = x * (1 - core) + y * core if q == 3 else at["xyz"[q]]
        mine = ring * 2 + core
        local[q] = [pltpu.make_async_copy(rows.at[q, mine], got.at[q, mine], own.at[q, 0]),
                    pltpu.make_async_copy(labels.at[q, mine], got_labels.at[q, mine], own.at[q, 1])]
        for copy in local[q]:
            copy.start()

    split_row = lax.broadcasted_iota(I32, (256, 256), 0)
    split_col = lax.broadcasted_iota(I32, (256, 256), 1)
    split = (split_col == (split_row % 128) * 2 + split_row // 128).astype(F32).astype(BF16)

    def add_up(q):
        def one(other_at, _):
            def add(src, total):
                name = got_labels[q, src, pl.ds(other_at, 1), :]
                parts = []
                for half in range(2):
                    block = got[q, src, other_at, half * 256:(half + 1) * 256, :]
                    flat = jnp.dot(split, block, preferred_element_type=F32).astype(BF16)
                    parts.append(jnp.concatenate([flat[:128], flat[128:]], axis=1))
                flat = jnp.concatenate(parts, axis=0)
                hit = (lax.broadcasted_iota(I32, (SUB, CAP), 0) == name).astype(F32).astype(BF16)
                return total + jnp.dot(hit, flat, preferred_element_type=F32)

            total = lax.fori_loop(0, 8, add, jnp.zeros((SUB, WIDTH), F32))
            if q == 0:
                for part in range(4):
                    partial[q, part, pl.ds(pl.multiple_of(other_at * 128, 128), 128), :] = total[part * 128:(part + 1) * 128]
            else:
                partial[q, other_at] = total
            return 0

        lax.fori_loop(0, 4, one, 0)

    second_axis = {0: "z", 1: "x", 2: "y"}
    second_copies = {}

    def start_second(q):
        here = y * (1 - core) + x * core if q == 3 else at[second_axis[q]]
        for distance in (2, 1, 3):
            device = by_core(distance) if q == 3 else along(second_axis[q], distance)
            copy = pltpu.make_async_remote_copy(
                src_ref=partial.at[q, (here + distance) % 4], dst_ref=got2.at[q, distance - 1],
                send_sem=s2.at[q, distance - 1], recv_sem=r2.at[q, distance - 1], device_id=device, device_id_type=MESH)
            copy.start()
            second_copies[q, distance] = copy

    third_axis = {0: "y", 1: "z", 2: "x", 3: "z"}
    third_copies = {}

    def start_third(q):
        here = y * (1 - core) + x * core if q == 3 else at[second_axis[q]]
        for distance in (2, 1, 3):
            second_copies[q, distance].wait()
        second[q] = partial[q, here] + got2[q, 0] + got2[q, 1] + got2[q, 2]
        here = at[third_axis[q]]
        for distance in (2, 1, 3):
            span = pl.ds(pl.multiple_of(((here + distance) % 4) * 128, 128), 128)
            copy = pltpu.make_async_remote_copy(
                src_ref=second.at[q, span], dst_ref=got3.at[q, distance - 1],
                send_sem=s3.at[q, distance - 1], recv_sem=r3.at[q, distance - 1],
                device_id=along(third_axis[q], distance), device_id_type=MESH)
            copy.start()
            third_copies[q, distance] = copy

    last_copies = {}

    def start_last(q):
        here = at[third_axis[q]]
        for distance in (2, 1, 3):
            third_copies[q, distance].wait()
        span = pl.ds(pl.multiple_of(here * 128, 128), 128)
        third[q] = second[q, span, :] + got3[q, 0] + got3[q, 1] + got3[q, 2]
        target = crossed.at[z] if q == 2 else out.at[pl.ds(pl.multiple_of(q * SUB + z * 128, 128), 128)]
        for distance in (2, 1, 3):
            copy = pltpu.make_async_remote_copy(
                src_ref=third.at[q], dst_ref=target, send_sem=s4.at[q, distance - 1], recv_sem=r4.at[q, distance - 1],
                device_id=along("z", distance), device_id_type=MESH)
            copy.start()
            last_copies[q, distance] = copy
        keep = pltpu.make_async_copy(third.at[q], target, own.at[q, 0])
        keep.start()
        last_copies[q, 0] = keep

    for q in (2, 0, 1, 3):
        for copy in local[q]:
            copy.wait()
        for j in range(len(hops)):
            for copy in first[q, j]:
                copy.wait()
        add_up(q)
        start_second(q)
    for q in (2, 0, 1, 3):
        start_third(q)
    for q in (2, 0, 1, 3):
        start_last(q)
    for distance in range(4):
        last_copies[2, distance].wait()
    spread = []
    target = out.at[pl.ds(pl.multiple_of(2 * SUB + x * 128, 128), 128)]
    for distance in (2, 1, 3):
        copy = pltpu.make_async_remote_copy(
            src_ref=crossed.at[(x + distance) % 4], dst_ref=target, send_sem=s5.at[distance - 1],
            recv_sem=r5.at[distance - 1], device_id=along("x", distance), device_id_type=MESH)
        copy.start()
        spread.append(copy)
    keep = pltpu.make_async_copy(crossed.at[x], target, own.at[2, 1])
    keep.start()
    spread.append(keep)
    for q in (0, 1, 3):
        for distance in range(4):
            last_copies[q, distance].wait()
    for copy in spread:
        copy.wait()


def reduce_call(rows, labels):
    dma = pltpu.SemaphoreType.DMA
    return pl.pallas_call(
        reduce_kernel,
        out_shape=jax.ShapeDtypeStruct((4 * SUB, WIDTH), F32),
        in_specs=[pl.BlockSpec(memory_space=pl.ANY)] * 2,
        out_specs=pl.BlockSpec(memory_space=pl.ANY),
        scratch_shapes=[
            pltpu.VMEM((4, 8, 4, 2 * CAP, 128), BF16),
            pltpu.VMEM((4, 8, 4, CAP), I32),
            pltpu.VMEM((4, 4, SUB, WIDTH), F32),
            pltpu.VMEM((4, 3, SUB, WIDTH), F32),
            pltpu.VMEM((4, SUB, WIDTH), F32),
            pltpu.VMEM((4, 3, 128, WIDTH), F32),
            pltpu.VMEM((4, 128, WIDTH), F32),
            pltpu.VMEM((4, 128, WIDTH), F32),
            dma((4, 7)), dma((4, 7)), dma((4, 7)), dma((4, 7)),
            dma((4, 3)), dma((4, 3)), dma((4, 3)), dma((4, 3)), dma((4, 3)), dma((4, 3)),
            dma((3,)), dma((3,)), dma((4, 2)),
        ],
        compiler_params=pltpu.CompilerParams(
            collective_id=0, has_side_effects=True, vmem_limit_bytes=56 << 20),
    )(rows, labels)


def local(embeddings, route, offset, centroids):
    slots, labels, counts, pairs = index_call(
        route.reshape(CHUNKS, CHUNK), offset.reshape(CHUNKS, CHUNK), embeddings)
    counts = lax.psum_scatter(counts.reshape(K), "cent", scatter_dimension=0, tiled=True)
    counts = lax.psum(counts, "sample")
    packed = place_call(slots.reshape(ROWS), pairs.reshape(ROWS, 2, 128))
    sums = reduce_call(packed.reshape(4, 8, 4, 2 * CAP, 128), labels.reshape(4, 8, 4, CAP))
    safe = jnp.maximum(counts, 1.0)
    return jnp.where(counts[:, None] > 0.0, sums / safe[:, None], centroids)


def solution(mesh):
    in_specs = (
        P(("sample", "cent"), None),
        P(("sample", "cent"), None),
        P(("sample", "cent")),
        P("cent", None),
    )
    return jax.shard_map(local, mesh=mesh, in_specs=in_specs, out_specs=P("cent", None), check_vma=False)
```

time: 552 us -> 263 us (0.48)
  the two profiles are of different devices: /device:TPU:0 before, /device:TPU:1 now
where the time goes in v1:
time: 263 us; the launch traced here: 262 us
  Pallas kernels  225 us (86%)
  between operations  14.2 us (5%)
  local copies, waits for them, and re-layouts  11.4 us (4%)
  blocking collectives  6.62 us (3%)
  other arithmetic  4.54 us (2%)
    pallas_call x1, Pallas kernels, reduce_call(): pl.pallas_call(reduce_kernel, out_shape=jax.ShapeDtypeStruct((4 * SUB, WI...  173 us
    pallas_call x1, Pallas kernels, place_call(): pl.pallas_call(place_kernel, out_shape=jax.ShapeDtypeStruct((SLOTS, 2, 12...  27 us
    pallas_call x1, Pallas kernels, index_call(): pl.pallas_call(index_kernel, grid=(CHUNKS,), out_shape=[jax.ShapeDtypeStr...  24.9 us
    unnamed x13, local copies, waits for them, and re-layouts  9.88 us
    psum x1, blocking collectives, local(): counts = lax.psum(counts, 'sample')  6.62 us
  transfers between devices with their start and end apart: 1, of which 0 were waited for; matrix products, arithmetic and copies ran while one was open for 1% of the time, Pallas kernels for 76%

profile of v1, /device:TPU:1, one launch (start us, length us, event | category | flops | bytes accessed | tf_op | source)
XLA Modules:
  0.0 262.2 jit_solution(9944087182691055138)
XLA Ops:
  6.5 0.0 all-reduce.3.cloned.1.call-start
  6.5 0.5 broadcast.6
  7.0 1.6 reduce.3
  8.7 0.9 reshape.25.offset
  9.6 0.0 copy-start.1
  9.6 3.4 %copy-done.1 = bf16[16384,256]{1,0:T(8,128)(2,1)S(1)} copy-done((bf16[16384,256]{1,0:T(8,128)(2,1)S(1)}, bf16[16384,256]{1,0:T(8,128)(2,1)}, u32[]{:S(2)}) %copy-start.1) | copy-done | bytes 8388632
  13.0 0.0 copy-start.3
  13.0 24.9 %shard_map.46 = (s32[32,512]{1,0:T(8,128)S(1)}, s32[128,256]{1,0:T(8,128)S(1)}, f32[128,512]{1,0:T(8,128)S(1)}, bf16[32768,128]{1,0:T(8,128)(2,1)S(1)}) custom-call(s32[32,512]{1,0:T(8,128)S(1)} %reshape.24.route, s32[32,512]{1,0:T(8,128)S(1)} %reshape.25.offset, bf16[16384,256]{1,0:T(8,128)(2,1)S(1)} %copy-done.1), custom_call_target="tpu_custom_call" | custom-call | tf_op jit(solution)/shard_map/pallas_call | solution.py:87
  37.9 0.0 copy-start
  37.9 3.2 %copy-done = bf16[32768,128]{1,0:T(8,128)(2,1)} copy-done((bf16[32768,128]{1,0:T(8,128)(2,1)}, bf16[32768,128]{1,0:T(8,128)(2,1)S(1)}, u32[]{:S(2)}) %copy-start) | copy-done | bytes 8388632
  41.1 0.8 copy.5
  41.9 0.0 all-reduce.3.cloned.1.call-update
  41.9 0.6 copy.6
  42.6 0.7 reshape.30.labels
  43.3 0.0 copy-done.3
  43.3 0.7 dynamic-slice
  44.6 27.0 %shard_map.47 = bf16[32768,2,128]{2,1,0:T(2,128)(2,1)} custom-call(s32[16384]{0:T(1024)} %bitcast.13, bf16[16384,2,128]{2,1,0:T(2,128)(2,1)} %bitcast.8), custom_call_target="tpu_custom_call" | custom-call | tf_op jit(solution)/shard_map/pallas_call | solution.py:150
  71.6 0.0 copy-start.2
  71.6 173.4 %shard_map.48 = f32[2048,256]{1,0:T(8,128)} custom-call(bf16[4,8,4,512,128]{4,3,2,1,0:T(8,128)(2,1)} %bitcast.11, s32[4,8,4,256]{3,2,1,0:T(4,128)} %reshape.30.labels), custom_call_target="tpu_custom_call" | custom-call | tf_op jit(solution)/shard_map/pallas_call | solution.py:336
  245.0 0.0 all-reduce.3.cloned.1.call-done
  245.1 0.7 dynamic-slice.1
  245.8 6.6 %psum.7 = f32[2048]{0:T(1024)S(1)} all-reduce(f32[2048]{0:T(1024)S(1)} %dynamic-slice.1), channel_id=1, replica_groups=mesh['sample'=4,'cent'=32] {'sample'}, use_global_device_ids=true, to_apply=%region_1.0 | all-reduce | flops 2048 | bytes 16384 | tf_op jit(solution)/shard_map/psum | solution.py:363
  252.4 0.0 copy-done.2
  252.4 2.9 %divide_select_fusion = f32[2048,256]{1,0:T(8,128)} fusion(f32[2048,256]{1,0:T(8,128)S(1)} %copy-done.2, f32[2048,256]{1,0:T(8,128)} %shard_map.48, f32[2048]{0:T(1024)S(1)} %broadcast_maximum_fusion, pred[2048]{0:T(1024)(128)(4,1)S(1)} %broadcast_compare_fusion), kind=kLoop, calls=%fused_computation | loop fusion | flops 1048576 | bytes 6301696 | tf_op jit(solution)/shard_map/jit(_where)/select_n | solution.py:367
  (3 shorter events, 0.0 us)
Async XLA Ops:
  6.5 238.5 %all-reduce.3.cloned.1.call-start = ((), (), s32[]{:S(2)}) async-start(), calls=%async_computation | async-start | bytes 524288
  9.6 3.4 %copy-start.1 = (bf16[16384,256]{1,0:T(8,128)(2,1)S(1)}, bf16[16384,256]{1,0:T(8,128)(2,1)}, u32[]{:S(2)}) copy-start(bf16[16384,256]{1,0:T(8,128)(2,1)} %x.1) | copy-start | bytes 25165828
  13.0 30.3 %copy-start.3 = (u32[128]{0:T(128)S(1)}, u32[128]{0:T(128)}, u32[]{:S(2)}) copy-start(u32[128]{0:T(128)} %constant.6) | copy-start | bytes 1540
  37.9 3.2 %copy-start = (bf16[32768,128]{1,0:T(8,128)(2,1)}, bf16[32768,128]{1,0:T(8,128)(2,1)S(1)}, u32[]{:S(2)}) copy-start(bf16[32768,128]{1,0:T(8,128)(2,1)S(1)} %get-tuple-element.11) | copy-start | bytes 25165828
  71.6 180.8 %copy-start.2 = (f32[2048,256]{1,0:T(8,128)S(1)}, f32[2048,256]{1,0:T(8,128)}, u32[]{:S(2)}) copy-start(f32[2048,256]{1,0:T(8,128)} %param.7) | copy-start | bytes 6291460
Sparse Core Ops, SparseCore 0:
  42.0 138.7 all-reduce.2

commit v2 on v0

v2 whole, which is shorter than its diff:
```python
import functools

import jax
import jax.numpy as jnp
from jax import lax
from jax.experimental import pallas as pl
from jax.experimental.pallas import tpu as pltpu
from jax.sharding import PartitionSpec as P

MESH = pl.DeviceIdType.MESH
K = 65536
WIDTH = 256
ROUTES = 128
SUB = 512
CAP = 256
ROWS = 16384
CHUNK = 1024
CHUNKS = ROWS // CHUNK
SLOTS = ROUTES * CAP
PART = 1024
F32, BF16, I32, I16 = jnp.float32, jnp.bfloat16, jnp.int32, jnp.int16
UNIT = 128


def place_of(route):
    quarter = route & 3
    core = (route >> 2) & 1
    y = (route >> 3) & 3
    x = route >> 5
    by_y = (quarter == 1) | ((quarter == 3) & (core == 1))
    ring = jnp.where(by_y, y, x)
    other = jnp.where(by_y, x, y)
    return quarter * 32 + ring * 8 + core * 4 + other


def pack_kernel(route, offset, x, packed_out, labels, rows, woven, packed, blank, slots, slots_s,
                upper, weave, base, found, in_sem, zero_sem, out_sem, slot_sem):
    def load(chunk):
        span = pl.ds(pl.multiple_of(chunk * CHUNK, CHUNK), CHUNK)
        return pltpu.make_async_copy(x.at[span], rows.at[span], in_sem.at[chunk])

    def clear(part):
        span = pl.ds(pl.multiple_of(part * PART, PART), PART)
        return pltpu.make_async_copy(blank, packed.at[span], zero_sem.at[part])

    def send(part):
        span = pl.ds(pl.multiple_of(part * PART, PART), PART)
        return pltpu.make_async_copy(packed.at[span], packed_out.at[span], out_sem.at[part])

    def slot_copy(turn):
        return pltpu.make_async_copy(slots.at[turn], slots_s.at[turn], slot_sem.at[turn])

    def each(count, act):
        def body(i, _):
            act(i)
            return 0
        lax.fori_loop(0, count, body, 0)

    blank[...] = jnp.zeros_like(blank)
    each(2, lambda i: load(i).start())
    each(SLOTS // PART, lambda i: clear(i).start())
    each(CHUNKS - 2, lambda i: load(i + 2).start())

    row = lax.broadcasted_iota(I32, (256, 256), 0)
    col = lax.broadcasted_iota(I32, (256, 256), 1)
    upper[...] = (row < col).astype(F32).astype(BF16)
    weave[...] = (col == (row >> 1) + (row & 1) * 128).astype(F32).astype(BF16)
    base[...] = jnp.zeros_like(base)
    found[...] = jnp.zeros_like(found)
    routes = lax.broadcasted_iota(I32, (ROUTES, CHUNK), 0)
    ranks = lax.broadcasted_iota(I32, (CHUNK, CAP), 1)

    def look(chunk, turn, between):
        at = pl.ds(chunk, 1)
        named = route[at, :]
        within = offset[at, :]
        place = place_of(named)
        mark = routes == place
        mark_f = mark.astype(F32)
        mark_b = mark_f.astype(BF16)
        between(0)
        start = base[:, :1]
        before = []
        for part in range(CHUNK // 256):
            cut = slice(part * 256, part * 256 + 256)
            before.append(jnp.dot(mark_b[:, cut], upper[...], preferred_element_type=F32) + start)
            start = start + jnp.sum(mark_f[:, cut], axis=1, keepdims=True)
        base[...] = jnp.broadcast_to(start, base.shape)
        rank = jnp.sum(jnp.where(mark, jnp.concatenate(before, axis=1), 0.0), axis=0, keepdims=True)
        slots[turn] = place * CAP + rank.astype(I32)
        between(1)
        for part in range(CHUNK // 256):
            first = pl.multiple_of(chunk * CHUNK + part * 256, 256)
            block = rows[pl.ds(first, 256), :]
            stacked = jnp.concatenate([
                jnp.concatenate([block[:128, :128], block[:128, 128:]], axis=0),
                jnp.concatenate([block[128:, :128], block[128:, 128:]], axis=0)], axis=1)
            mixed = jnp.dot(weave[...], stacked, preferred_element_type=F32).astype(BF16)
            woven[turn, part * 512:part * 512 + 256, :] = mixed[:, :128]
            woven[turn, part * 512 + 256:part * 512 + 512, :] = mixed[:, 128:]
            if part % 2:
                between(2 + part // 2)
        lines = jnp.concatenate([rank, within.astype(F32), jnp.zeros((6, CHUNK), F32)], axis=0)
        columns = lines.T
        within_f = columns[:, 1:2]
        value = jnp.where(ranks == columns[:, 0:1].astype(I32), within_f - 256.0, 0.0).astype(BF16)
        between(4)
        found[...] += jnp.dot(mark_b, value, preferred_element_type=F32)
        between(5)
        between(6)
        between(7)

    def move(turn, piece):
        for j in range(piece * (CHUNK // 8), (piece + 1) * (CHUNK // 8)):
            packed[slots_s[turn, 0, j]] = woven[turn, 2 * j:2 * j + 2, :]

    def ahead(chunk, _):
        load(chunk).wait()
        look(chunk, chunk, lambda piece: None)
        slot_copy(chunk).start()
        return 0

    def both(chunk, _):
        load(chunk).wait()
        turn = chunk % 3
        old = (chunk + 1) % 3
        slot_copy(old).wait()
        look(chunk, turn, lambda piece: move(old, piece))
        slot_copy(turn).start()
        return 0

    def behind(chunk, _):
        old = chunk % 3
        slot_copy(old).wait()

        for piece in range(8):
            move(old, piece)
        return 0

    lax.fori_loop(0, 2, ahead, 0)
    each(SLOTS // PART, lambda i: clear(i).wait())
    lax.fori_loop(2, CHUNKS, both, 0)
    lax.fori_loop(CHUNKS - 2, CHUNKS, behind, 0)
    each(SLOTS // PART, lambda i: send(i).start())
    lanes = lax.broadcasted_iota(I32, (ROUTES, CAP), 1)
    labels[...] = jnp.where(lanes < base[:, :1].astype(I32), found[...].astype(I32) + 256, -1)
    each(SLOTS // PART, lambda i: send(i).wait())


def pack_call(route, offset, x):
    vmem = pl.BlockSpec(memory_space=pltpu.VMEM)
    hbm = pl.BlockSpec(memory_space=pl.ANY)
    dma = pltpu.SemaphoreType.DMA
    return pl.pallas_call(
        pack_kernel,
        out_shape=[
            jax.ShapeDtypeStruct((SLOTS, 2, 128), BF16),
            jax.ShapeDtypeStruct((ROUTES, CAP), I32),
        ],
        in_specs=[vmem, vmem, hbm],
        out_specs=[hbm, vmem],
        scratch_shapes=[
            pltpu.VMEM((ROWS, WIDTH), BF16),
            pltpu.VMEM((3, 2 * CHUNK, 128), BF16),
            pltpu.VMEM((SLOTS, 2, 128), BF16),
            pltpu.VMEM((PART, 2, 128), BF16),
            pltpu.VMEM((3, 1, CHUNK), I32),
            pltpu.SMEM((3, 1, CHUNK), I32),
            pltpu.VMEM((256, 256), BF16),
            pltpu.VMEM((256, 256), BF16),
            pltpu.VMEM((ROUTES, 128), F32),
            pltpu.VMEM((ROUTES, CAP), F32),
            dma((CHUNKS,)), dma((SLOTS // PART,)), dma((SLOTS // PART,)), dma((3,)),
        ],
        compiler_params=pltpu.CompilerParams(vmem_limit_bytes=60 << 20),
    )(route, offset, x)


def device_at(x, y, z, core):
    return {"sample": z, "cent": (x * 4 + y) * 2 + core}


def encode(ref, value, count):
    eye = lax.broadcasted_iota(I32, (UNIT, UNIT), 0) == lax.broadcasted_iota(I32, (UNIT, UNIT), 1)
    top = jnp.max(jnp.abs(value), axis=1, keepdims=True)
    level = jnp.ceil(jnp.log2(jnp.maximum(top, 2.0 ** -90)) * 256.0) + 1.0
    ref[:UNIT, :] = jnp.round(value * (jnp.exp2(level * (-1.0 / 256.0)) * 32767.0)).astype(I32).astype(I16)
    line = jnp.sum(jnp.where(eye, level, 0.0), axis=0, keepdims=True)
    both = jnp.concatenate([line, count], axis=1)
    ref[UNIT:, :] = jnp.broadcast_to(both, (16, WIDTH)).astype(I32).astype(I16)


def upright(line):
    eye = lax.broadcasted_iota(I32, (UNIT, UNIT), 0) == lax.broadcasted_iota(I32, (UNIT, UNIT), 1)
    return jnp.sum(jnp.where(eye, line, 0.0), axis=1, keepdims=True)


def decode(ref):
    last = ref[UNIT:, :].astype(I32).astype(F32)
    level = upright(last[0:1, :UNIT])
    return ref[:UNIT, :].astype(I32).astype(F32) * (jnp.exp2(level * (1.0 / 256.0)) * (1.0 / 32767.0)), last[0:1, UNIT:]


def reduce_kernel(rows, labels, centroids, out, got, got_labels, total_s, count_s, kept, kept_count, sent2, got2,
                  sent3, got3, got4, got5, old, s1, r1, sl, rl, s2, r2, s3, r3, s4, r4, s5, r5, own, old_sem):
    z = lax.axis_index("sample")
    cent = lax.axis_index("cent")
    x, y, core = cent // 8, (cent // 2) % 4, cent % 2
    at = {"x": x, "y": y, "z": z}

    def along(axis, distance, core_to=None):
        to = dict(at)
        to[axis] = (to[axis] + distance) % 4
        return device_at(to["x"], to["y"], to["z"], core if core_to is None else core_to)

    def by_core(distance):
        return device_at((x + distance * core) % 4, (y + distance * (1 - core)) % 4, z, core)

    barrier = pltpu.get_barrier_semaphore()
    other = (core + 1) % 2
    pl.semaphore_signal(barrier, inc=1, device_id=device_at(x, y, z, other), device_id_type=MESH)
    for axis in "xyz":
        for distance in (1, 2, 3):
            for core_to in (core, other):
                pl.semaphore_signal(barrier, inc=1, device_id=along(axis, distance, core_to), device_id_type=MESH)
    pl.semaphore_wait(barrier, 19)

    hops = [(2, 0), (2, 1), (1, 0), (3, 0), (1, 1), (3, 1), (0, 1)]

    def first_copy(src, dst, ss, rs, q, j, step=None):
        distance, flip = hops[j]
        core_to = (core + flip) % 2
        if q == 3:
            ring = x * (1 - core_to) + y * core_to
            other_at = y * (1 - core_to) + x * core_to
            device = device_at((x + distance * (1 - core_to)) % 4, (y + distance * core_to) % 4, z, core_to)
        else:
            ring = at["xyz"[q]]
            other_at = at["yxy"[q]]
            device = along("xyz"[q], distance, core_to)
        to = ((ring + distance) % 4) * 2 + core_to
        mine = ring * 2 + core
        if step is None:
            src, dst, ss, rs = src.at[q, to], dst.at[q, mine], ss.at[q, j], rs.at[q, j]
        else:
            block = (other_at + step + 1) % 4
            src, dst, ss, rs = src.at[q, to, block], dst.at[q, mine, block], ss.at[q, j, step], rs.at[q, j, step]
        return pltpu.make_async_remote_copy(
            src_ref=src, dst_ref=dst, send_sem=ss, recv_sem=rs, device_id=device, device_id_type=MESH)

    def row_copy(q, j, step):
        return first_copy(rows, got, s1, r1, q, j, step)

    def label_copy(q, j):
        return first_copy(labels, got_labels, sl, rl, q, j)

    def start_rows(q, step):
        for j in range(len(hops)):
            row_copy(q, j, step).start()

    every = (0, 1, 2, 3)
    for q in every:
        for j in range(len(hops)):
            label_copy(q, j).start()

    def start_three(step, _):
        for q in (0, 1, 2):
            start_rows(q, step)
        return 0

    def start_fourth(step, _):
        start_rows(3, step)
        return 0

    lax.fori_loop(0, 4, start_three, 0)
    local = {}
    for q in every:
        ring = x * (1 - core) + y * core if q == 3 else at["xyz"[q]]
        mine = ring * 2 + core
        local[q] = [pltpu.make_async_copy(rows.at[q, mine], got.at[q, mine], own.at[q, 0]),
                    pltpu.make_async_copy(labels.at[q, mine], got_labels.at[q, mine], own.at[q, 1])]
        for copy in local[q]:
            copy.start()

    split_row = lax.broadcasted_iota(I32, (256, 256), 0)
    split_col = lax.broadcasted_iota(I32, (256, 256), 1)
    split = (split_col == (split_row % 128) * 2 + split_row // 128).astype(F32).astype(BF16)
    centroid = lax.broadcasted_iota(I32, (SUB, CAP), 0)
    eye = lax.broadcasted_iota(I32, (UNIT, UNIT), 0) == lax.broadcasted_iota(I32, (UNIT, UNIT), 1)
    second_axis = {0: "z", 1: "x", 2: "y"}
    second_at = {0: z, 1: x, 2: y, 3: y * (1 - core) + x * core}

    def second_copy(q, step, distance, block):
        if q == 0:
            src, dst = sent2.at[q, (z + distance) % 4, block], got2.at[q, distance - 1, block]
            number, device = distance - 1, along("z", distance)
        else:
            src, dst, number = sent2.at[q, step], got2.at[q, step], 0
            device = by_core(distance) if q == 3 else along(second_axis[q], distance)
        return pltpu.make_async_remote_copy(
            src_ref=src, dst_ref=dst, send_sem=s2.at[q, step, number], recv_sem=r2.at[q, step, number],
            device_id=device, device_id_type=MESH)

    def block_of(q, step):
        return ((y if q == 0 else second_at[q]) + step + 1) % 4

    def add_up(q, step):
        for j in range(len(hops)):
            row_copy(q, j, step).wait()
        block = block_of(q, step)
        flats, hits, tally = [], [], None
        for src in range(8):
            for half in range(2):
                both = jnp.dot(split, got[q, src, block, half * 256:(half + 1) * 256, :], preferred_element_type=F32).astype(BF16)
                flats.append(jnp.concatenate([both[:128], both[128:]], axis=1))
            name = got_labels[q, src, pl.ds(block, 1), :]
            hit = (centroid == name).astype(F32)
            tally = hit if tally is None else tally + hit
            hits.append(hit.astype(BF16))
        total_s[...] = jnp.dot(
            jnp.concatenate(hits, axis=1), jnp.concatenate(flats, axis=0), preferred_element_type=F32)
        column = jnp.sum(tally, axis=1, keepdims=True)
        for part in range(4):
            count = jnp.sum(jnp.where(eye, column[part * UNIT:(part + 1) * UNIT], 0.0), axis=0, keepdims=True)
            count_s[part] = jnp.broadcast_to(count, (8, UNIT))
        if q == 0:
            for part in range(4):
                encode(sent2.at[q, part, block], total_s[part * UNIT:(part + 1) * UNIT, :], count_s[part, 0:1, :])
            kept[q, block] = total_s[pl.ds(pl.multiple_of(z * UNIT, UNIT), UNIT), :]
            kept_count[q, block] = count_s[z]
            for distance in (2, 1, 3):
                second_copy(q, step, distance, block).start()
        else:
            @pl.when(step < 3)
            def _():
                for part in range(4):
                    encode(sent2.at[q, step, part], total_s[part * UNIT:(part + 1) * UNIT, :], count_s[part, 0:1, :])
                second_copy(q, step, step + 1, block).start()

            @pl.when(step == 3)
            def _():
                for part in range(4):
                    kept[q, part] = total_s[part * UNIT:(part + 1) * UNIT, :]
                    kept_count[q, part] = count_s[part]

    third_axis = {0: "y", 1: "z", 2: "x", 3: "z"}
    third_copies = {}

    def start_third(q):
        if q == 0:
            for step in range(4):
                for distance in (2, 1, 3):
                    second_copy(q, step, distance, block_of(q, step)).wait()
        else:
            for step in range(3):
                second_copy(q, step, step + 1, block_of(q, step)).wait()

        def join(part, _):
            value, count = kept[q, part], kept_count[q, part]
            for source in range(3):
                more, number = decode(got2.at[q, source, part])
                value, count = value + more, count + number
            kept[q, part] = value
            kept_count[q, part] = count
            encode(sent3.at[q, part], value, count[0:1, :])
            return 0

        lax.fori_loop(0, 4, join, 0)
        here = at[third_axis[q]]
        for distance in (2, 1, 3):
            copy = pltpu.make_async_remote_copy(
                src_ref=sent3.at[q, (here + distance) % 4], dst_ref=got3.at[q, distance - 1],
                send_sem=s3.at[q, distance - 1], recv_sem=r3.at[q, distance - 1],
                device_id=along(third_axis[q], distance), device_id_type=MESH)
            copy.start()
            third_copies[q, distance] = copy

    last_copies = {}

    def start_last(q):
        here = at[third_axis[q]]
        for distance in (2, 1, 3):
            third_copies[q, distance].wait()
        value, count = kept[q, here], kept_count[q, here]
        for source in range(3):
            more, number = decode(got3.at[q, source])
            value, count = value + more, count + number
        count = count[0:1, :]
        encode(got4.at[q, z], value / jnp.maximum(upright(count), 1.0), jnp.minimum(count, 1.0))
        for distance in (2, 1, 3):
            copy = pltpu.make_async_remote_copy(
                src_ref=got4.at[q, z], dst_ref=got4.at[q, z], send_sem=s4.at[q, distance - 1],
                recv_sem=r4.at[q, distance - 1], device_id=along("z", distance), device_id_type=MESH)
            copy.start()
            last_copies[q, distance] = copy

    spread = []

    def start_spread():
        for distance in (1, 2, 3):
            last_copies[2, distance].wait()
        for distance in (2, 1, 3):
            copy = pltpu.make_async_remote_copy(
                src_ref=got4.at[2, (x + distance) % 4], dst_ref=got5.at[x], send_sem=s5.at[distance - 1],
                recv_sem=r5.at[distance - 1], device_id=along("x", distance), device_id_type=MESH)
            copy.start()
            spread.append(copy)
        got5[x] = got4[2, x]

    def finish(q):
        if q == 2:
            for copy in spread:
                copy.wait()
        else:
            for distance in (1, 2, 3):
                last_copies[q, distance].wait()

        def part_out(part, _):
            value, count = decode(got5.at[part] if q == 2 else got4.at[q, part])
            span = pl.ds(pl.multiple_of(q * SUB + part * UNIT, UNIT), UNIT)
            out[span, :] = jnp.where(upright(count) > 0.0, value, old[span, :])
            return 0

        lax.fori_loop(0, 4, part_out, 0)

    old_copy = pltpu.make_async_copy(centroids, old, old_sem)
    old_copy.start()
    for q in every:
        for copy in local[q]:
            copy.wait()
        for j in range(len(hops)):
            label_copy(q, j).wait()

    def add_three(step, _):
        for q in (0, 1, 2):
            add_up(q, step)

        @pl.when(step == 2)
        def _():
            lax.fori_loop(0, 4, start_fourth, 0)

        return 0

    def add_fourth(step, _):
        add_up(3, step)
        return 0

    lax.fori_loop(0, 4, add_three, 0)
    lax.fori_loop(0, 1, add_fourth, 0)
    for q in (2, 0, 1):
        start_third(q)
    lax.fori_loop(1, 3, add_fourth, 0)
    for q in (2, 0, 1):
        start_last(q)
    lax.fori_loop(3, 4, add_fourth, 0)
    start_spread()
    old_copy.wait()
    start_third(3)
    finish(0)
    finish(1)
    start_last(3)
    finish(2)
    finish(3)


def reduce_call(rows, labels, centroids):
    dma = pltpu.SemaphoreType.DMA
    any_space = pl.BlockSpec(memory_space=pl.ANY)
    return pl.pallas_call(
        reduce_kernel,
        out_shape=jax.ShapeDtypeStruct((4 * SUB, WIDTH), F32),
        in_specs=[any_space] * 3,
        out_specs=pl.BlockSpec(memory_space=pltpu.VMEM),
        scratch_shapes=[
            pltpu.VMEM((4, 8, 4, 2 * CAP, 128), BF16),
            pltpu.VMEM((4, 8, 4, CAP), I32),
            pltpu.VMEM((SUB, WIDTH), F32),
            pltpu.VMEM((4, 8, UNIT), F32),
            pltpu.VMEM((4, 4, UNIT, WIDTH), F32),
            pltpu.VMEM((4, 4, 8, UNIT), F32),
            pltpu.VMEM((4, 4, 4, UNIT + 16, WIDTH), I16),
            pltpu.VMEM((4, 3, 4, UNIT + 16, WIDTH), I16),
            pltpu.VMEM((4, 4, UNIT + 16, WIDTH), I16),
            pltpu.VMEM((4, 3, UNIT + 16, WIDTH), I16),
            pltpu.VMEM((4, 4, UNIT + 16, WIDTH), I16),
            pltpu.VMEM((4, UNIT + 16, WIDTH), I16),
            pltpu.VMEM((4 * SUB, WIDTH), F32),
            dma((4, 7, 4)), dma((4, 7, 4)), dma((4, 7)), dma((4, 7)),
            dma((4, 4, 3)), dma((4, 4, 3)), dma((4, 3)), dma((4, 3)), dma((4, 3)), dma((4, 3)),
            dma((3,)), dma((3,)), dma((4, 2)), dma,
        ],
        compiler_params=pltpu.CompilerParams(
            collective_id=0, has_side_effects=True, vmem_limit_bytes=60 << 20),
    )(rows, labels, centroids)


def local(embeddings, route, offset, centroids):
    packed, labels = pack_call(
        route.reshape(CHUNKS, CHUNK), offset.reshape(CHUNKS, CHUNK), embeddings)
    return reduce_call(packed.reshape(4, 8, 4, 2 * CAP, 128), labels.reshape(4, 8, 4, CAP), centroids)


def solution(mesh):
    in_specs = (
        P(("sample", "cent"), None),
        P(("sample", "cent"), None),
        P(("sample", "cent")),
        P("cent", None),
    )
    return jax.shard_map(local, mesh=mesh, in_specs=in_specs, out_specs=P("cent", None), check_vma=False)
```

time: 552 us -> 165 us (0.30)
  waiting for transfers between devices: 310 us -> 0 us
  Pallas kernels: 0 us -> 155 us
  local copies, waits for them, and re-layouts: 157 us -> 7.25 us
  other arithmetic: 29.1 us -> 1.64 us
  starting transfers between devices: 15 us -> 0 us
  between operations: 14.2 us -> 0.02 us
  matrix products: 13.3 us -> 0 us
  blocking collectives: 11.9 us -> 0 us
    all_to_all x2 -> x0, waiting for transfers between devices: 241 us -> none  [the longest x1 241 us: local(): lax.all_to_all(buffer, 'cent', split_axis=0, concat_axis=0, tiled=True)]
    pallas_call x0 -> x2, Pallas kernels: none -> 155 us  [the longest x1 121 us: reduce_call(): pl.pallas_call(reduce_kernel, out_shape=jax.ShapeDtypeStruct((4 * SUB, WI...]
    scatter x2 -> x0, local copies, waits for them, and re-layouts: 140 us -> none  [the longest x1 78.5 us: fill_slots(): buffer = jnp.zeros((total, width), jnp.bfloat16).at[slots].set(embeddings)]
    reduce_scatter x1 -> x0, waiting for transfers between devices: 38.2 us -> none  [local(): lax.psum_scatter(partial_value.reshape(n_sample * sub, width), 'sample',...]
    all_gather x1 -> x0, waiting for transfers between devices: 30.8 us -> none  [local(): return lax.all_gather(fresh, 'sample', axis=0, tiled=True)]
    reduce_sum x2 -> x0, other arithmetic: 16.3 us -> none  [the longest x1 8.31 us: ranks_within(): return jnp.sum(running * marks, axis=1)]
    all_to_all x2 -> x0, starting transfers between devices: 14.9 us -> none  [the longest x1 7.51 us: local(): lax.all_to_all(buffer, 'cent', split_axis=0, concat_axis=0, tiled=True)]
    dot_general x1 -> x0, matrix products: 13.3 us -> none  [local(): jnp.einsum('ansk,ansd->nkd', onehot, got_rows, preferred_element_type=jnp...]
  transfers between devices with their start and end apart: 4 -> 0, of which waited for: 3 -> 0; matrix products, arithmetic and copies ran while one was open for 16% -> 0% of each run, Pallas kernels for 0% -> 0%
where the time goes in v2:
time: 165 us; the launch traced here: 164 us
  Pallas kernels  155 us (94%)
  local copies, waits for them, and re-layouts  7.25 us (4%)
    pallas_call x1, Pallas kernels, reduce_call(): pl.pallas_call(reduce_kernel, out_shape=jax.ShapeDtypeStruct((4 * SUB, WI...  121 us
    pallas_call x1, Pallas kernels, pack_call(): pl.pallas_call(pack_kernel, out_shape=[jax.ShapeDtypeStruct((SLOTS, 2, 12...  34.2 us
    unnamed x2, local copies, waits for them, and re-layouts  3.56 us

profile of v2, /device:TPU:0, one launch (start us, length us, event | category | flops | bytes accessed | tf_op | source)
XLA Modules:
  0.0 163.8 jit_solution(5384058944117422946)
XLA Ops:
  0.0 0.5 broadcast.3
  0.5 1.6 %reduce.3 = s32[16384]{0:T(1024)S(1)} reduce(s32[16384,1]{0,1:T(1,128)} %param.5, s32[]{:T(128)} %broadcast.3), dimensions={1}, to_apply=%param.5.reduce_sub_computation.3 | reduce | bytes 131076 | tf_op args[1]
  2.2 0.6 reshape.12.route
  2.8 1.5 reshape.13.offset
  4.3 34.2 %shard_map.46 = (bf16[32768,2,128]{2,1,0:T(2,128)(2,1)}, s32[128,256]{1,0:T(8,128)}) custom-call(s32[16,1024]{1,0:T(8,128)} %reshape.12.route, s32[16,1024]{1,0:T(8,128)} %reshape.13.offset, bf16[16384,256]{1,0:T(8,128)(2,1)} %x.1), custom_call_target="tpu_custom_call" | custom-call | tf_op jit(solution)/shard_map/pallas_call | solution.py:154
  38.5 1.6 reshape.15.labels
  40.1 120.7 %shard_map.47 = f32[2048,256]{1,0:T(8,128)} custom-call(bf16[4,8,4,512,128]{4,3,2,1,0:T(8,128)(2,1)} %bitcast.2, s32[4,8,4,256]{3,2,1,0:T(4,128)} %reshape.15.labels, f32[2048,256]{1,0:T(8,128)} %centroids.1), custom_call_target="tpu_custom_call" | custom-call | tf_op jit(solution)/shard_map/pallas_call | solution.py:469
  160.8 3.0 %copy.6 = f32[2048,256]{1,0:T(8,128)} copy(f32[2048,256]{1,0:T(8,128)} %shard_map.47) | data formatting | bytes 4194304

commit v3 on v2

--- a/solution.py
+++ b/solution.py
@@ -33,8 +33,8 @@
     return quarter * 32 + ring * 8 + core * 4 + other
 
 
-def pack_kernel(route, offset, x, packed_out, labels, rows, woven, packed, blank, slots, slots_s,
-                upper, weave, base, found, in_sem, zero_sem, out_sem, slot_sem):
+def pack_kernel(route, offset, x, packed, labels, rows, woven, woven1, blank, slots, slots1, slots_s,
+                slots_s1, upper, weave, base, found, in_sem, zero_sem, slot_sem):
     def load(chunk):
         span = pl.ds(pl.multiple_of(chunk * CHUNK, CHUNK), CHUNK)
         return pltpu.make_async_copy(x.at[span], rows.at[span], in_sem.at[chunk])
@@ -43,12 +43,10 @@
         span = pl.ds(pl.multiple_of(part * PART, PART), PART)
         return pltpu.make_async_copy(blank, packed.at[span], zero_sem.at[part])
 
-    def send(part):
-        span = pl.ds(pl.multiple_of(part * PART, PART), PART)
-        return pltpu.make_async_copy(packed.at[span], packed_out.at[span], out_sem.at[part])
+    pairs, places, places_s = (woven, woven1), (slots, slots1), (slots_s, slots_s1)
 
     def slot_copy(turn):
-        return pltpu.make_async_copy(slots.at[turn], slots_s.at[turn], slot_sem.at[turn])
+        return pltpu.make_async_copy(places[turn], places_s[turn], slot_sem.at[turn])
 
     def each(count, act):
         def body(i, _):
@@ -70,10 +68,20 @@
     routes = lax.broadcasted_iota(I32, (ROUTES, CHUNK), 0)
     ranks = lax.broadcasted_iota(I32, (CHUNK, CAP), 1)
 
+    def interleave(chunk, turn, part):
+        first = pl.multiple_of(chunk * CHUNK + part * 256, 256)
+        block = rows[pl.ds(first, 256), :]
+        stacked = jnp.concatenate([
+            jnp.concatenate([block[:128, :128], block[:128, 128:]], axis=0),
+            jnp.concatenate([block[128:, :128], block[128:, 128:]], axis=0)], axis=1)
+        mixed = jnp.dot(weave[...], stacked, preferred_element_type=F32).astype(BF16)
+        pairs[turn][part * 512:part * 512 + 256, :] = mixed[:, :128]
+        pairs[turn][part * 512 + 256:part * 512 + 512, :] = mixed[:, 128:]
+
     def look(chunk, turn, between):
-        at = pl.ds(chunk, 1)
-        named = route[at, :]
-        within = offset[at, :]
+        at = pl.ds(pl.multiple_of(chunk * CHUNK, CHUNK), CHUNK)
+        named = route[:, at]
+        within = offset[:, at]
         place = place_of(named)
         mark = routes == place
         mark_f = mark.astype(F32)
@@ -87,64 +95,57 @@
             start = start + jnp.sum(mark_f[:, cut], axis=1, keepdims=True)
         base[...] = jnp.broadcast_to(start, base.shape)
         rank = jnp.sum(jnp.where(mark, jnp.concatenate(before, axis=1), 0.0), axis=0, keepdims=True)
-        slots[turn] = place * CAP + rank.astype(I32)
+        places[turn][...] = place * CAP + rank.astype(I32)
         between(1)
-        for part in range(CHUNK // 256):
-            first = pl.multiple_of(chunk * CHUNK + part * 256, 256)
-            block = rows[pl.ds(first, 256), :]
-            stacked = jnp.concatenate([
-                jnp.concatenate([block[:128, :128], block[:128, 128:]], axis=0),
-                jnp.concatenate([block[128:, :128], block[128:, 128:]], axis=0)], axis=1)
-            mixed = jnp.dot(weave[...], stacked, preferred_element_type=F32).astype(BF16)
-            woven[turn, part * 512:part * 512 + 256, :] = mixed[:, :128]
-            woven[turn, part * 512 + 256:part * 512 + 512, :] = mixed[:, 128:]
-            if part % 2:
-                between(2 + part // 2)
         lines = jnp.concatenate([rank, within.astype(F32), jnp.zeros((6, CHUNK), F32)], axis=0)
         columns = lines.T
+        between(2)
         within_f = columns[:, 1:2]
         value = jnp.where(ranks == columns[:, 0:1].astype(I32), within_f - 256.0, 0.0).astype(BF16)
-        between(4)
+        between(3)
         found[...] += jnp.dot(mark_b, value, preferred_element_type=F32)
-        between(5)
-        between(6)
-        between(7)
 
     def move(turn, piece):
         for j in range(piece * (CHUNK // 8), (piece + 1) * (CHUNK // 8)):
-            packed[slots_s[turn, 0, j]] = woven[turn, 2 * j:2 * j + 2, :]
-
-    def ahead(chunk, _):
+            packed[places_s[turn][0, j]] = pairs[turn][2 * j:2 * j + 2, :]
+
+    def full(chunk, turn):
         load(chunk).wait()
-        look(chunk, chunk, lambda piece: None)
-        slot_copy(chunk).start()
+        slot_copy(turn).wait()
+
+        def between(piece):
+            move(turn, piece * 2)
+            interleave(chunk - 1, 1 - turn, piece)
+            move(turn, piece * 2 + 1)
+
+        look(chunk, turn, between)
+        slot_copy(turn).start()
+
+    def two(i, _):
+        full(2 * i, 0)
+        full(2 * i + 1, 1)
         return 0
 
-    def both(chunk, _):
-        load(chunk).wait()
-        turn = chunk % 3
-        old = (chunk + 1) % 3
-        slot_copy(old).wait()
-        look(chunk, turn, lambda piece: move(old, piece))
-        slot_copy(turn).start()
-        return 0
-
-    def behind(chunk, _):
-        old = chunk % 3
-        slot_copy(old).wait()
-
-        for piece in range(8):
-            move(old, piece)
-        return 0
-
-    lax.fori_loop(0, 2, ahead, 0)
+    load(0).wait()
+    look(0, 0, lambda piece: None)
+    slot_copy(0).start()
+    load(1).wait()
+    look(1, 1, lambda piece: interleave(0, 0, piece))
+    slot_copy(1).start()
     each(SLOTS // PART, lambda i: clear(i).wait())
-    lax.fori_loop(2, CHUNKS, both, 0)
-    lax.fori_loop(CHUNKS - 2, CHUNKS, behind, 0)
-    each(SLOTS // PART, lambda i: send(i).start())
+    lax.fori_loop(1, CHUNKS // 2, two, 0)
+    slot_copy(0).wait()
+    for piece in range(8):
+        if piece < 4:
+            interleave(CHUNKS - 1, 1, piece)
+        move(0, piece)
+    slot_copy(1).wait()
+    for piece in range(8):
+        move(1, piece)
     lanes = lax.broadcasted_iota(I32, (ROUTES, CAP), 1)
-    labels[...] = jnp.where(lanes < base[:, :1].astype(I32), found[...].astype(I32) + 256, -1)
-    each(SLOTS // PART, lambda i: send(i).wait())
+    named = jnp.where(lanes < base[:, :1].astype(I32), found[...].astype(I32) + 256, -1)
+    for four in range(ROUTES // 4):
+        labels[four] = named[four * 4:four * 4 + 4, :]
 
 
 def pack_call(route, offset, x):
@@ -154,25 +155,27 @@
     return pl.pallas_call(
         pack_kernel,
         out_shape=[
-            jax.ShapeDtypeStruct((SLOTS, 2, 128), BF16),
-            jax.ShapeDtypeStruct((ROUTES, CAP), I32),
+            pltpu.VMEM((SLOTS, 2, 128), BF16),
+            jax.ShapeDtypeStruct((ROUTES // 4, 4, CAP), I32),
         ],
         in_specs=[vmem, vmem, hbm],
-        out_specs=[hbm, vmem],
+        out_specs=[vmem, vmem],
         scratch_shapes=[
             pltpu.VMEM((ROWS, WIDTH), BF16),
-            pltpu.VMEM((3, 2 * CHUNK, 128), BF16),
-            pltpu.VMEM((SLOTS, 2, 128), BF16),
+            pltpu.VMEM((2 * CHUNK, 128), BF16),
+            pltpu.VMEM((2 * CHUNK, 128), BF16),
             pltpu.VMEM((PART, 2, 128), BF16),
-            pltpu.VMEM((3, 1, CHUNK), I32),
-            pltpu.SMEM((3, 1, CHUNK), I32),
+            pltpu.VMEM((1, CHUNK), I32),
+            pltpu.VMEM((1, CHUNK), I32),
+            pltpu.SMEM((1, CHUNK), I32),
+            pltpu.SMEM((1, CHUNK), I32),
             pltpu.VMEM((256, 256), BF16),
             pltpu.VMEM((256, 256), BF16),
             pltpu.VMEM((ROUTES, 128), F32),
             pltpu.VMEM((ROUTES, CAP), F32),
-            dma((CHUNKS,)), dma((SLOTS // PART,)), dma((SLOTS // PART,)), dma((3,)),
+            dma((CHUNKS,)), dma((SLOTS // PART,)), dma((2,)),
         ],
-        compiler_params=pltpu.CompilerParams(vmem_limit_bytes=60 << 20),
+        compiler_params=pltpu.CompilerParams(vmem_limit_bytes=40 << 20),
     )(route, offset, x)
 
 
@@ -201,7 +204,7 @@
     return ref[:UNIT, :].astype(I32).astype(F32) * (jnp.exp2(level * (1.0 / 256.0)) * (1.0 / 32767.0)), last[0:1, UNIT:]
 
 
-def reduce_kernel(rows, labels, centroids, out, got, got_labels, total_s, count_s, kept, kept_count, sent2, got2,
+def reduce_kernel(rows, labels, centroids, out, got, got_labels, hits, flats, total_s, count_s, kept, kept_count, sent2, got2,
                   sent3, got3, got4, got5, old, s1, r1, sl, rl, s2, r2, s3, r3, s4, r4, s5, r5, own, old_sem):
     z = lax.axis_index("sample")
     cent = lax.axis_index("cent")
@@ -287,43 +290,42 @@
     split = (split_col == (split_row % 128) * 2 + split_row // 128).astype(F32).astype(BF16)
     centroid = lax.broadcasted_iota(I32, (SUB, CAP), 0)
     eye = lax.broadcasted_iota(I32, (UNIT, UNIT), 0) == lax.broadcasted_iota(I32, (UNIT, UNIT), 1)
-    second_axis = {0: "z", 1: "x", 2: "y"}
-    second_at = {0: z, 1: x, 2: y, 3: y * (1 - core) + x * core}
+    second_at = {2: y, 3: y * (1 - core) + x * core}
 
     def second_copy(q, step, distance, block):
-        if q == 0:
+        if q < 2:
             src, dst = sent2.at[q, (z + distance) % 4, block], got2.at[q, distance - 1, block]
             number, device = distance - 1, along("z", distance)
         else:
             src, dst, number = sent2.at[q, step], got2.at[q, step], 0
-            device = by_core(distance) if q == 3 else along(second_axis[q], distance)
+            device = by_core(distance) if q == 3 else along("y", distance)
         return pltpu.make_async_remote_copy(
             src_ref=src, dst_ref=dst, send_sem=s2.at[q, step, number], recv_sem=r2.at[q, step, number],
             device_id=device, device_id_type=MESH)
 
     def block_of(q, step):
-        return ((y if q == 0 else second_at[q]) + step + 1) % 4
+        return ((at["yx"[q]] if q < 2 else second_at[q]) + step + 1) % 4
 
     def add_up(q, step):
         for j in range(len(hops)):
             row_copy(q, j, step).wait()
         block = block_of(q, step)
-        flats, hits, tally = [], [], None
+        tally = None
         for src in range(8):
             for half in range(2):
                 both = jnp.dot(split, got[q, src, block, half * 256:(half + 1) * 256, :], preferred_element_type=F32).astype(BF16)
-                flats.append(jnp.concatenate([both[:128], both[128:]], axis=1))
+                first = src * CAP + half * 128
+                flats[first:first + 128, :] = jnp.concatenate([both[:128], both[128:]], axis=1)
             name = got_labels[q, src, pl.ds(block, 1), :]
             hit = (centroid == name).astype(F32)
             tally = hit if tally is None else tally + hit
-            hits.append(hit.astype(BF16))
-        total_s[...] = jnp.dot(
-            jnp.concatenate(hits, axis=1), jnp.concatenate(flats, axis=0), preferred_element_type=F32)
+            hits[:, src * CAP:(src + 1) * CAP] = hit.astype(BF16)
+        total_s[...] = jnp.dot(hits[...], flats[...], preferred_element_type=F32)
         column = jnp.sum(tally, axis=1, keepdims=True)
         for part in range(4):
             count = jnp.sum(jnp.where(eye, column[part * UNIT:(part + 1) * UNIT], 0.0), axis=0, keepdims=True)
             count_s[part] = jnp.broadcast_to(count, (8, UNIT))
-        if q == 0:
+        if q < 2:
             for part in range(4):
                 encode(sent2.at[q, part, block], total_s[part * UNIT:(part + 1) * UNIT, :], count_s[part, 0:1, :])
             kept[q, block] = total_s[pl.ds(pl.multiple_of(z * UNIT, UNIT), UNIT), :]
@@ -343,11 +345,11 @@
                     kept[q, part] = total_s[part * UNIT:(part + 1) * UNIT, :]
                     kept_count[q, part] = count_s[part]
 
-    third_axis = {0: "y", 1: "z", 2: "x", 3: "z"}
+    third_axis = {0: "y", 1: "x", 2: "x", 3: "z"}
     third_copies = {}
 
     def start_third(q):
-        if q == 0:
+        if q < 2:
             for step in range(4):
                 for distance in (2, 1, 3):
                     second_copy(q, step, distance, block_of(q, step)).wait()
@@ -468,12 +470,14 @@
     any_space = pl.BlockSpec(memory_space=pl.ANY)
     return pl.pallas_call(
         reduce_kernel,
-        out_shape=jax.ShapeDtypeStruct((4 * SUB, WIDTH), F32),
-        in_specs=[any_space] * 3,
+        out_shape=pltpu.VMEM((4 * SUB, WIDTH), F32),
+        in_specs=[pl.BlockSpec(memory_space=pltpu.VMEM), any_space, any_space],
         out_specs=pl.BlockSpec(memory_space=pltpu.VMEM),
         scratch_shapes=[
             pltpu.VMEM((4, 8, 4, 2 * CAP, 128), BF16),
             pltpu.VMEM((4, 8, 4, CAP), I32),
+            pltpu.VMEM((SUB, 8 * CAP), BF16),
+            pltpu.VMEM((8 * CAP, WIDTH), BF16),
             pltpu.VMEM((SUB, WIDTH), F32),
             pltpu.VMEM((4, 8, UNIT), F32),
             pltpu.VMEM((4, 4, UNIT, WIDTH), F32),
@@ -490,14 +494,15 @@
             dma((3,)), dma((3,)), dma((4, 2)), dma,
         ],
         compiler_params=pltpu.CompilerParams(
-            collective_id=0, has_side_effects=True, vmem_limit_bytes=60 << 20),
+            collective_id=0, has_side_effects=True, vmem_limit_bytes=44 << 20),
     )(rows, labels, centroids)
 
 
 def local(embeddings, route, offset, centroids):
     packed, labels = pack_call(
-        route.reshape(CHUNKS, CHUNK), offset.reshape(CHUNKS, CHUNK), embeddings)
-    return reduce_call(packed.reshape(4, 8, 4, 2 * CAP, 128), labels.reshape(4, 8, 4, CAP), centroids)
+        route.T, offset.reshape(1, ROWS), embeddings)
+    packed = pltpu.with_memory_space_constraint(packed.reshape(4, 8, 4, 2 * CAP, 128), pltpu.VMEM)
+    return reduce_call(packed, labels.reshape(4, 8, 4, CAP), centroids)
 
 
 def solution(mesh):

time: 165 us -> 140 us (0.85)
  Pallas kernels: 155 us -> 139 us
  local copies, waits for them, and re-layouts: 7.25 us -> 1.32 us
    pallas_call x2, Pallas kernels: 155 us -> 139 us  [the longest x1 115 us: reduce_call(): pl.pallas_call(reduce_kernel, out_shape=pltpu.VMEM((4 * SUB, WIDTH), F32)...]
    reshape x3 -> x0, local copies, waits for them, and re-layouts: 3.69 us -> none  [the longest x1 1.58 us: local(): labels.reshape(4, 8, 4, CAP)]
    unnamed x2 -> x1, local copies, waits for them, and re-layouts: 3.56 us -> 1.32 us
where the time goes in v3:
time: 140 us
  Pallas kernels  139 us (99%)
    pallas_call x1, Pallas kernels, reduce_call(): pl.pallas_call(reduce_kernel, out_shape=pltpu.VMEM((4 * SUB, WIDTH), F32)...  115 us
    pallas_call x1, Pallas kernels, pack_call(): pl.pallas_call(pack_kernel, out_shape=[pltpu.VMEM((SLOTS, 2, 128), BF16),...  24 us

profile of v3, /device:TPU:0, one launch (start us, length us, event | category | flops | bytes accessed | tf_op | source)
XLA Modules:
  0.0 140.2 jit_solution(10284201846054144815)
XLA Ops:
  0.0 24.0 %shard_map.46 = (bf16[32768,2,128]{2,1,0:T(2,128)(2,1)S(1)}, s32[32,4,256]{2,1,0:T(4,128)}) custom-call(s32[1,16384]{1,0:T(1,128)} %bitcast.6, s32[1,16384]{1,0:T(1,128)} %bitcast.7, bf16[16384,256]{1,0:T(8,128)(2,1)} %x.1), custom_call_target="tpu_custom_call" | custom-call | tf_op jit(solution)/shard_map/pallas_call | solution.py:155
  24.0 115.0 %shard_map.47 = f32[2048,256]{1,0:T(8,128)S(1)} custom-call(bf16[4,8,4,512,128]{4,3,2,1,0:T(8,128)(2,1)S(1)} %bitcast.4, s32[4,8,4,256]{3,2,1,0:T(4,128)} %bitcast.5, f32[2048,256]{1,0:T(8,128)} %centroids.1), custom_call_target="tpu_custom_call" | custom-call | tf_op jit(solution)/shard_map/pallas_call | solution.py:471
  138.9 1.3 copy.6

commit v4 on v3

--- a/solution.py
+++ b/solution.py
@@ -14,7 +14,7 @@
 SUB = 512
 CAP = 256
 ROWS = 16384
-CHUNK = 1024
+CHUNK = 2048
 CHUNKS = ROWS // CHUNK
 SLOTS = ROUTES * CAP
 PART = 1024
@@ -115,7 +115,8 @@
 
         def between(piece):
             move(turn, piece * 2)
-            interleave(chunk - 1, 1 - turn, piece)
+            for part in range(piece * CHUNK // 1024, (piece + 1) * CHUNK // 1024):
+                interleave(chunk - 1, 1 - turn, part)
             move(turn, piece * 2 + 1)
 
         look(chunk, turn, between)
@@ -130,14 +131,15 @@
     look(0, 0, lambda piece: None)
     slot_copy(0).start()
     load(1).wait()
-    look(1, 1, lambda piece: interleave(0, 0, piece))
+    look(1, 1, lambda piece: [interleave(0, 0, part) for part in range(piece * CHUNK // 1024, (piece + 1) * CHUNK // 1024)])
     slot_copy(1).start()
     each(SLOTS // PART, lambda i: clear(i).wait())
     lax.fori_loop(1, CHUNKS // 2, two, 0)
     slot_copy(0).wait()
     for piece in range(8):
         if piece < 4:
-            interleave(CHUNKS - 1, 1, piece)
+            for part in range(piece * CHUNK // 1024, (piece + 1) * CHUNK // 1024):
+                interleave(CHUNKS - 1, 1, part)
         move(0, piece)
     slot_copy(1).wait()
     for piece in range(8):

time: 140 us -> 138 us (0.986)
  Pallas kernels: 139 us -> 137 us
    pallas_call x1, Pallas kernels: 24 us -> 21.7 us  [pack_call(): pl.pallas_call(pack_kernel, out_shape=[pltpu.VMEM((SLOTS, 2, 128), BF16),...]
where the time goes in v4:
time: 138 us
  Pallas kernels  137 us (99%)
    pallas_call x1, Pallas kernels, reduce_call(): pl.pallas_call(reduce_kernel, out_shape=pltpu.VMEM((4 * SUB, WIDTH), F32)...  115 us
    pallas_call x1, Pallas kernels, pack_call(): pl.pallas_call(pack_kernel, out_shape=[pltpu.VMEM((SLOTS, 2, 128), BF16),...  21.7 us

profile of v4, /device:TPU:0, one launch (start us, length us, event | category | flops | bytes accessed | tf_op | source)
XLA Modules:
  0.0 138.0 jit_solution(6713262252184815390)
XLA Ops:
  0.0 21.7 %shard_map.46 = (bf16[32768,2,128]{2,1,0:T(2,128)(2,1)S(1)}, s32[32,4,256]{2,1,0:T(4,128)}) custom-call(s32[1,16384]{1,0:T(1,128)} %bitcast.6, s32[1,16384]{1,0:T(1,128)} %bitcast.7, bf16[16384,256]{1,0:T(8,128)(2,1)} %x.1), custom_call_target="tpu_custom_call" | custom-call | tf_op jit(solution)/shard_map/pallas_call | solution.py:157
  21.7 115.0 %shard_map.47 = f32[2048,256]{1,0:T(8,128)S(1)} custom-call(bf16[4,8,4,512,128]{4,3,2,1,0:T(8,128)(2,1)S(1)} %bitcast.4, s32[4,8,4,256]{3,2,1,0:T(4,128)} %bitcast.5, f32[2048,256]{1,0:T(8,128)} %centroids.1), custom_call_target="tpu_custom_call" | custom-call | tf_op jit(solution)/shard_map/pallas_call | solution.py:473
  136.7 1.3 copy.6
